TPU v7x, 256 devices: a whole 4x4x8 slice. The times are simulated.
256 devices in a mesh: dp: 16 (over z, core), comp: 16 (over y, x).
Axes of the slice: x: 4, y: 4, z: 8, core: 2. Of those that a mesh axis runs over, the one named last changes fastest.
Arguments:
- points: bfloat16 [524288, 768], P(('dp', 'comp')), may hold values from -6 to 6
- candidates: int32 [4096, 4], P(('dp', 'comp')), may hold values from 0 to 511, as said below
- means: bfloat16 [65536, 768], P(('dp', 'comp')), may hold values from -0.59765625 to 0.59765625
- inv_var: bfloat16 [65536, 768], P(('dp', 'comp')), may hold values from 0.5 to 1.5
- log_weight: bfloat16 [65536], P(('dp', 'comp')), may hold values from -12 to -9
Outputs:
- counts: float32 [65536], P(('dp', 'comp'))
- first_moment: float32 [65536, 768], P(('dp', 'comp'))
- second_moment: float32 [65536, 768], P(('dp', 'comp'))
- loglik: float32 [524288], P(('dp', 'comp'))
Inputs may be any that keep to these rules, and one draw needn't show every extreme that they name: `candidates`: each row block names 4 different component blocks; all blocks b named by the row blocks of device index i along dp+comp satisfy (b // 2) % 16 == i % 16, that is, one owner group serves each device's rows.
All inputs are finite; a program needn't handle non-finite values.
Results may differ from a plain program's by a relative error of at most 0.028.
Values may be sent and summed in bfloat16 or wider, within the bound.
A program may use at most 128 MiB of HBM per device.

v0:
```python
import math

import jax
import jax.numpy as jnp
from jax import lax
from jax.sharding import PartitionSpec as P

CB = 128
RB = 128
CANDS = 4


def component_consts(mean_values, inv_values, log_values):
    feature_count = mean_values.shape[1]
    mean_f = mean_values.astype(jnp.float32)
    inv_f = inv_values.astype(jnp.float32)
    return (
        log_values.astype(jnp.float32)
        + 0.5 * jnp.sum(jnp.log(inv_f), axis=1)
        - 0.5 * jnp.sum(inv_f * mean_f * mean_f, axis=1)
        - 0.5 * feature_count * math.log(2.0 * math.pi)
    )


def block_terms(row_block, selector, scaled_flat, inverse_flat, constants):
    group_rows, slot_count, block_total = selector.shape
    feature_count = row_block.shape[2]
    row_f = row_block.astype(jnp.float32)
    squares = (row_f * row_f).astype(jnp.bfloat16)
    pick = selector.reshape(group_rows * slot_count, block_total)
    pick_bf = pick.astype(jnp.bfloat16)
    chosen_scaled = jnp.dot(pick_bf, scaled_flat, preferred_element_type=jnp.float32).astype(
        jnp.bfloat16
    )
    chosen_inverse = jnp.dot(pick_bf, inverse_flat, preferred_element_type=jnp.float32).astype(
        jnp.bfloat16
    )
    chosen_scaled = chosen_scaled.reshape(group_rows, slot_count, CB, feature_count)
    chosen_inverse = chosen_inverse.reshape(group_rows, slot_count, CB, feature_count)
    chosen_consts = jnp.dot(pick, constants, precision=lax.Precision.HIGHEST).reshape(
        group_rows, slot_count, CB
    )
    linear = jnp.einsum(
        "grd,gskd->grsk", row_block, chosen_scaled, preferred_element_type=jnp.float32
    )
    quadratic = jnp.einsum(
        "grd,gskd->grsk", squares, chosen_inverse, preferred_element_type=jnp.float32
    )
    densities = chosen_consts[:, None] + linear - 0.5 * quadratic
    row_peak = jnp.max(densities, axis=(2, 3))
    normalizer = row_peak + jnp.log(
        jnp.sum(jnp.exp(densities - row_peak[:, :, None, None]), axis=(2, 3))
    )
    responsibility = jnp.exp(densities - normalizer[:, :, None, None]).astype(jnp.bfloat16)
    counts = jnp.sum(responsibility.astype(jnp.float32), axis=1)
    first_moment = jnp.einsum(
        "grsk,grd->gskd", responsibility, row_block, preferred_element_type=jnp.float32
    )
    second_moment = jnp.einsum(
        "grsk,grd->gskd", responsibility, squares, preferred_element_type=jnp.float32
    )
    return (normalizer, counts, first_moment, second_moment)


def on_device(points, candidates, means, inv_var, log_weight):
    feature_count = points.shape[1]
    owner_count = lax.axis_size("comp")
    held_blocks = means.shape[0] // CB
    all_means, all_inverse, all_logs = (
        lax.all_gather(means, "dp", axis=0, tiled=True),
        lax.all_gather(inv_var, "dp", axis=0, tiled=True),
        lax.all_gather(log_weight, "dp", axis=0, tiled=True),
    )
    all_scaled = (all_inverse.astype(jnp.float32) * all_means.astype(jnp.float32)).astype(
        jnp.bfloat16
    )
    all_consts = component_consts(all_means, all_inverse, all_logs)
    group_blocks = all_scaled.shape[0] // CB
    scaled_flat = all_scaled.reshape(group_blocks, CB * feature_count)
    inverse_flat = all_inverse.reshape(group_blocks, CB * feature_count)
    constants = all_consts.reshape(group_blocks, CB)
    local_ids = candidates // (owner_count * held_blocks) * held_blocks + candidates % held_blocks
    block_count = candidates.shape[0]
    row_groups = points.reshape(block_count // 4, 4, RB, feature_count)
    id_groups = local_ids.reshape(block_count // 4, 4, CANDS)
    block_iota = jnp.arange(group_blocks, dtype=jnp.int32)

    def accumulate(running, inputs):
        row_block, chosen_ids = inputs
        selector = (chosen_ids[:, :, None] == block_iota[None, None, :]).astype(jnp.float32)
        normalizer, counts, first_part, second_part = block_terms(
            row_block, selector, scaled_flat, inverse_flat, constants
        )
        spread = selector.reshape(-1, group_blocks).T
        slot_total = spread.shape[1]
        new_counts = jnp.dot(
            spread, counts.reshape(slot_total, CB), precision=lax.Precision.HIGHEST
        )
        new_first = jnp.dot(
            spread,
            first_part.reshape(slot_total, CB * feature_count),
            precision=lax.Precision.HIGHEST,
        )
        new_second = jnp.dot(
            spread,
            second_part.reshape(slot_total, CB * feature_count),
            precision=lax.Precision.HIGHEST,
        )
        running = (running[0] + new_counts, running[1] + new_first, running[2] + new_second)
        return (running, normalizer)

    initial = (
        jnp.zeros((group_blocks, CB), jnp.float32),
        jnp.zeros((group_blocks, CB * feature_count), jnp.float32),
        jnp.zeros((group_blocks, CB * feature_count), jnp.float32),
    )
    partials, normalizers = lax.scan(accumulate, initial, (row_groups, id_groups))
    count_sum, first_sum, second_sum = (
        lax.psum_scatter(
            partials[0].astype(jnp.bfloat16), "dp", scatter_dimension=0, tiled=True
        ).astype(jnp.float32),
        lax.psum_scatter(
            partials[1].astype(jnp.bfloat16), "dp", scatter_dimension=0, tiled=True
        ).astype(jnp.float32),
        lax.psum_scatter(
            partials[2].astype(jnp.bfloat16), "dp", scatter_dimension=0, tiled=True
        ).astype(jnp.float32),
    )
    loglik = normalizers.reshape(-1) / feature_count
    return (
        count_sum.reshape(-1),
        first_sum.reshape(-1, feature_count),
        second_sum.reshape(-1, feature_count),
        loglik,
    )


def solution(mesh):
    return jax.shard_map(
        on_device,
        mesh=mesh,
        in_specs=(
            P(("dp", "comp"), None),
            P(("dp", "comp"), None),
            P(("dp", "comp"), None),
            P(("dp", "comp"), None),
            P(("dp", "comp")),
        ),
        out_specs=(
            P(("dp", "comp")),
            P(("dp", "comp"), None),
            P(("dp", "comp"), None),
            P(("dp", "comp")),
        ),
        check_vma=False,
    )
```

profile of v0, /device:TPU:1, one launch (start us, length us, event | category | flops | bytes accessed | tf_op | source)
XLA Modules:
  0.0 519.7 jit_solution(4086402239218131101)
XLA Ops:
  7.2 0.7 all-gather.4.cloned.1.call-update
  7.9 0.7 all-gather.6.cloned.1.call-update
  9.4 21.3 %all-gather = bf16[16,1,256]{2,1,0:T(2,128)(2,1)S(1)} all-gather(bf16[1,1,256]{2,1,0:T(2,128)(2,1)S(1)} %reshape.127), channel_id=1, replica_groups=mesh['dp'=16,'comp'=16] {'dp'}, dimensions={0}, use_global_device_ids=true | all-gather | bytes 8704 | tf_op jit(solution)/shard_map/all_gather | solution.py:72
  30.7 0.7 fusion.36
  31.5 28.7 %all-gather.4.cloned.1.call-done = bf16[4096,768]{1,0:T(8,128)(2,1)} async-done(((bf16[256,768]{1,0:T(8,128)(2,1)}), bf16[4096,768]{1,0:T(8,128)(2,1)}) %all-gather.4.cloned.1.call-update) | async-done | bytes 6291472 | tf_op jit(solution)/shard_map/all_gather | solution.py:71
  60.1 46.5 %all-gather.6.cloned.1.call-done = bf16[4096,768]{1,0:T(8,128)(2,1)} async-done(((bf16[256,768]{1,0:T(8,128)(2,1)}), bf16[4096,768]{1,0:T(8,128)(2,1)}) %all-gather.6.cloned.1.call-update) | async-done | bytes 6291472 | tf_op jit(solution)/shard_map/all_gather | solution.py:70
  106.6 10.6 %fusion.32 = (f32[4096]{0:T(1024)S(1)}, f32[4096]{0:T(1024)S(1)}, bf16[4096,768]{1,0:T(8,128)(2,1)}) fusion(bf16[4096,768]{1,0:T(8,128)(2,1)} %all-gather.4.cloned.1.call-done, bf16[4096,768]{1,0:T(8,128)(2,1)} %all-gather.6.cloned.1.call-done), kind=kLoop, calls=%fused_computation.46 | loop fusion | flops 22011904 | bytes 18907136 | tf_op jit(solution)/shard_map/reduce_sum | solution.py:19
  117.2 7.2 %reshape.109 = bf16[32,98304]{1,0:T(8,128)(2,1)} reshape(bf16[4096,768]{1,0:T(8,128)(2,1)} %get-tuple-element.182) | data formatting | bytes 12582912 | tf_op jit(solution)/shard_map/reshape | solution.py:79
  124.5 7.3 %reshape.110 = bf16[32,98304]{1,0:T(8,128)(2,1)} reshape(bf16[4096,768]{1,0:T(8,128)(2,1)} %all-gather.4.cloned.1.call-done) | data formatting | bytes 12582912 | tf_op jit(solution)/shard_map/reshape | solution.py:80
  131.8 203.8 %while.18 = (s32[]{:T(128)}, f32[32,128]{1,0:T(8,128)S(1)}, f32[32,98304]{1,0:T(8,128)}, f32[32,98304]{1,0:T(8,128)}, f32[4,4,128]{2,1,0:T(4,128)S(1)}, /*index=...) while((s32[]{:T(128)}, f32[32,128]{1,0:T(8,128)S(1)}, ...), condition=%wide.region_6.7_spmd.clone.clone, body=%wide.region_2.6_spmd.clone.clone.sunk | while | flops 3042191872 | bytes 255429680 | solution.py:117
  131.9 4.0 convolution_convert_fusion.4
  135.9 0.7 copy.22
  136.8 2.1 convolution_add_fusion.6
  138.9 1.0 convolution_convert_fusion.5
  140.6 2.1 fusion.90
  143.3 2.1 fusion.92
  145.4 6.3 %copy.24 = f32[2,8,128,768]{3,1,2,0:T(8,128)} copy(f32[2,8,128,768]{3,2,1,0:T(8,128)S(1)} %bitcast.122) | data formatting | bytes 12582912 | tf_op jit(solution)/shard_map/while
  151.7 10.6 %convolution_add_fusion.7 = f32[32,98304]{1,0:T(8,128)} fusion(f32[16,98304]{1,0:T(8,128)} %bitcast.119, f32[32,98304]{1,0:T(8,128)} %get-tuple-element.272, pred[]{:T(512)S(6)} %compare.6, s32[16]{0:T(128)S(1)} %eq.108), kind=kOutput, calls=%fused_computation.2.clone.1 | convolution fusion | flops 610271744 | bytes 31457344 | tf_op jit(solution)/shard_map/while/body/eval_jaxpr/dot_general | solution.py:99
  162.4 2.3 fusion.93
  164.6 3.6 copy.25
  168.3 8.2 %convolution_add_fusion.8 = f32[32,98304]{1,0:T(8,128)S(1)} fusion(f32[16,98304]{1,0:T(8,128)S(1)} %bitcast.120, f32[32,98304]{1,0:T(8,128)S(1)} %bitcast.126, pred[]{:T(512)S(6)} %compare.6, s32[16]{0:T(128)S(1)} %eq.108), kind=kOutput, calls=%fused_computation.1.clone.1 | convolution fusion | flops 610271744 | bytes 31457344 | tf_op jit(solution)/shard_map/while/body/eval_jaxpr/dot_general | solution.py:104
  176.5 4.5 copy-done
  181.4 4.0 convolution_convert_fusion.4
  186.3 2.1 convolution_add_fusion.6
  188.4 1.0 convolution_convert_fusion.5
  190.2 2.1 fusion.90
  192.9 2.1 fusion.92
  195.0 6.3 %copy.24 = f32[2,8,128,768]{3,1,2,0:T(8,128)} copy(f32[2,8,128,768]{3,2,1,0:T(8,128)S(1)} %bitcast.122) | data formatting | bytes 12582912 | tf_op jit(solution)/shard_map/while
  201.3 12.5 %convolution_add_fusion.7 = f32[32,98304]{1,0:T(8,128)} fusion(f32[16,98304]{1,0:T(8,128)} %bitcast.119, f32[32,98304]{1,0:T(8,128)} %get-tuple-element.272, pred[]{:T(512)S(6)} %compare.6, s32[16]{0:T(128)S(1)} %eq.108), kind=kOutput, calls=%fused_computation.2.clone.1 | convolution fusion | flops 610271744 | bytes 31457344 | tf_op jit(solution)/shard_map/while/body/eval_jaxpr/dot_general | solution.py:99
  213.7 2.3 fusion.93
  216.0 3.6 copy.25
  219.7 8.2 %convolution_add_fusion.8 = f32[32,98304]{1,0:T(8,128)S(1)} fusion(f32[16,98304]{1,0:T(8,128)S(1)} %bitcast.120, f32[32,98304]{1,0:T(8,128)S(1)} %bitcast.126, pred[]{:T(512)S(6)} %compare.6, s32[16]{0:T(128)S(1)} %eq.108), kind=kOutput, calls=%fused_computation.1.clone.1 | convolution fusion | flops 610271744 | bytes 31457344 | tf_op jit(solution)/shard_map/while/body/eval_jaxpr/dot_general | solution.py:104
  227.9 4.5 copy-done
  232.8 4.0 convolution_convert_fusion.4
  236.7 0.7 copy.22
  237.7 2.1 convolution_add_fusion.6
  239.8 1.0 convolution_convert_fusion.5
  241.5 2.1 fusion.90
  244.2 2.1 fusion.92
  246.3 6.3 %copy.24 = f32[2,8,128,768]{3,1,2,0:T(8,128)} copy(f32[2,8,128,768]{3,2,1,0:T(8,128)S(1)} %bitcast.122) | data formatting | bytes 12582912 | tf_op jit(solution)/shard_map/while
  252.6 12.5 %convolution_add_fusion.7 = f32[32,98304]{1,0:T(8,128)} fusion(f32[16,98304]{1,0:T(8,128)} %bitcast.119, f32[32,98304]{1,0:T(8,128)} %get-tuple-element.272, pred[]{:T(512)S(6)} %compare.6, s32[16]{0:T(128)S(1)} %eq.108), kind=kOutput, calls=%fused_computation.2.clone.1 | convolution fusion | flops 610271744 | bytes 31457344 | tf_op jit(solution)/shard_map/while/body/eval_jaxpr/dot_general | solution.py:99
  265.1 2.3 fusion.93
  267.4 3.6 copy.25
  271.0 8.2 %convolution_add_fusion.8 = f32[32,98304]{1,0:T(8,128)S(1)} fusion(f32[16,98304]{1,0:T(8,128)S(1)} %bitcast.120, f32[32,98304]{1,0:T(8,128)S(1)} %bitcast.126, pred[]{:T(512)S(6)} %compare.6, s32[16]{0:T(128)S(1)} %eq.108), kind=kOutput, calls=%fused_computation.1.clone.1 | convolution fusion | flops 610271744 | bytes 31457344 | tf_op jit(solution)/shard_map/while/body/eval_jaxpr/dot_general | solution.py:104
  279.2 4.5 copy-done
  284.1 4.0 convolution_convert_fusion.4
  288.1 0.7 copy.22
  289.0 2.1 convolution_add_fusion.6
  291.2 1.0 convolution_convert_fusion.5
  292.9 2.1 fusion.90
  295.6 2.1 fusion.92
  297.7 6.3 %copy.24 = f32[2,8,128,768]{3,1,2,0:T(8,128)} copy(f32[2,8,128,768]{3,2,1,0:T(8,128)S(1)} %bitcast.122) | data formatting | bytes 12582912 | tf_op jit(solution)/shard_map/while
  304.0 12.5 %convolution_add_fusion.7 = f32[32,98304]{1,0:T(8,128)} fusion(f32[16,98304]{1,0:T(8,128)} %bitcast.119, f32[32,98304]{1,0:T(8,128)} %get-tuple-element.272, pred[]{:T(512)S(6)} %compare.6, s32[16]{0:T(128)S(1)} %eq.108), kind=kOutput, calls=%fused_computation.2.clone.1 | convolution fusion | flops 610271744 | bytes 31457344 | tf_op jit(solution)/shard_map/while/body/eval_jaxpr/dot_general | solution.py:99
  316.5 2.3 fusion.93
  318.7 3.6 copy.25
  322.4 8.2 %convolution_add_fusion.8 = f32[32,98304]{1,0:T(8,128)S(1)} fusion(f32[16,98304]{1,0:T(8,128)S(1)} %bitcast.120, f32[32,98304]{1,0:T(8,128)S(1)} %bitcast.126, pred[]{:T(512)S(6)} %compare.6, s32[16]{0:T(128)S(1)} %eq.108), kind=kOutput, calls=%fused_computation.1.clone.1 | convolution fusion | flops 610271744 | bytes 31457344 | tf_op jit(solution)/shard_map/while/body/eval_jaxpr/dot_general | solution.py:104
  330.6 4.5 copy-done
  335.6 7.9 %convert_element_type.56 = bf16[32,98304]{1,0:T(8,128)(2,1)} convert(f32[32,98304]{1,0:T(8,128)} %get-tuple-element.68) | non-fusion elementwise | flops 3145728 | bytes 18874368 | tf_op jit(solution)/shard_map/convert_element_type | solution.py:123
  343.5 7.9 %convert_element_type.57 = bf16[32,98304]{1,0:T(8,128)(2,1)} convert(f32[32,98304]{1,0:T(8,128)} %get-tuple-element.69) | non-fusion elementwise | flops 3145728 | bytes 18874368 | tf_op jit(solution)/shard_map/convert_element_type | solution.py:126
  353.2 24.3 %all-reduce = bf16[32,128]{1,0:T(8,128)(2,1)S(1)} all-reduce(bf16[32,128]{1,0:T(8,128)(2,1)S(1)} %convert_element_type.55), channel_id=2, replica_groups=mesh['dp'=16,'comp'=16] {'dp'}, use_global_device_ids=true, to_apply=%region_7.8.clone | all-reduce | flops 4096 | bytes 16384
  378.7 128.9 %all-reduce.6.cloned.1.call-done = (bf16[32,98304]{1,0:T(8,128)(2,1)}, bf16[32,98304]{1,0:T(8,128)(2,1)}) async-done(((bf16[32,98304]{1,0:T(8,128)(2,1)}, bf16[32,98304]{1,0:T(8,128)(2,1)}), (bf16[32,98304]{1,0:T(8,128)(2,1)}, bf16[32,98304]{1,0:T(8,128)(2,1)})) %all-reduce.6.cloned.1.call-update) | async-done | bytes 12582928
  507.6 2.5 dynamic-slice_convert_fusion
  510.0 1.6 reshape.124
  511.6 1.6 reshape.126
  (107 shorter events, 11.3 us)
Async XLA Ops:
  7.2 53.0 %all-gather.4.cloned.1.call-start = ((), (), s32[]{:S(2)}) async-start(), calls=%async_computation | async-start | bytes 6684672 | tf_op jit(solution)/shard_map/all_gather | solution.py:71
  7.9 98.7 %all-gather.6.cloned.1.call-start = ((), (), s32[]{:S(2)}) async-start(), calls=%async_computation.1 | async-start | bytes 6684672 | tf_op jit(solution)/shard_map/all_gather | solution.py:70
  8.6 498.9 %all-reduce.6.cloned.1.call-start = ((), (), s32[]{:S(2)}) async-start(), calls=%async_computation.2 | async-start | bytes 25165824
  131.9 7.0 %slice-start.3 = ((s8[6291456]{0:T(1024)(128)(4,1)}), s8[4194304]{0:T(1024)(128)(4,1)S(1)}, s32[]{:S(2)}) async-start(s8[6291456]{0:T(1024)(128)(4,1)} %bitcast.129), calls=%async_computation.6 | async-start | bytes 8388608 | tf_op jit(solution)/shard_map/while
  135.8 3.1 slice-start.4
  151.7 16.6 %slice-start = ((s8[12582912]{0:T(1024)(128)(4,1)}), s8[4194304]{0:T(1024)(128)(4,1)S(1)}, s32[]{:S(2)}) async-start(s8[12582912]{0:T(1024)(128)(4,1)} %bitcast.125), calls=%async_computation.3 | async-start | bytes 8388608 | tf_op jit(solution)/shard_map/while
  151.7 16.6 %slice-start.1 = ((s8[12582912]{0:T(1024)(128)(4,1)}), s8[4194304]{0:T(1024)(128)(4,1)S(1)}, s32[]{:S(2)}) async-start(s8[12582912]{0:T(1024)(128)(4,1)} %bitcast.125), calls=%async_computation.4 | async-start | bytes 8388608 | tf_op jit(solution)/shard_map/while
  162.4 5.9 %slice-start.2 = ((s8[12582912]{0:T(1024)(128)(4,1)}), s8[4194304]{0:T(1024)(128)(4,1)S(1)}, s32[]{:S(2)}) async-start(s8[12582912]{0:T(1024)(128)(4,1)} %bitcast.125), calls=%async_computation.5 | async-start | bytes 8388608 | tf_op jit(solution)/shard_map/while
  176.5 4.5 copy-start
  181.4 7.0 %slice-start.3 = ((s8[6291456]{0:T(1024)(128)(4,1)}), s8[4194304]{0:T(1024)(128)(4,1)S(1)}, s32[]{:S(2)}) async-start(s8[6291456]{0:T(1024)(128)(4,1)} %bitcast.129), calls=%async_computation.6 | async-start | bytes 8388608 | tf_op jit(solution)/shard_map/while
  185.4 3.1 slice-start.4
  201.3 18.4 %slice-start = ((s8[12582912]{0:T(1024)(128)(4,1)}), s8[4194304]{0:T(1024)(128)(4,1)S(1)}, s32[]{:S(2)}) async-start(s8[12582912]{0:T(1024)(128)(4,1)} %bitcast.125), calls=%async_computation.3 | async-start | bytes 8388608 | tf_op jit(solution)/shard_map/while
  201.3 18.4 %slice-start.1 = ((s8[12582912]{0:T(1024)(128)(4,1)}), s8[4194304]{0:T(1024)(128)(4,1)S(1)}, s32[]{:S(2)}) async-start(s8[12582912]{0:T(1024)(128)(4,1)} %bitcast.125), calls=%async_computation.4 | async-start | bytes 8388608 | tf_op jit(solution)/shard_map/while
  213.7 5.9 %slice-start.2 = ((s8[12582912]{0:T(1024)(128)(4,1)}), s8[4194304]{0:T(1024)(128)(4,1)S(1)}, s32[]{:S(2)}) async-start(s8[12582912]{0:T(1024)(128)(4,1)} %bitcast.125), calls=%async_computation.5 | async-start | bytes 8388608 | tf_op jit(solution)/shard_map/while
  227.9 4.5 copy-start
  232.8 7.0 %slice-start.3 = ((s8[6291456]{0:T(1024)(128)(4,1)}), s8[4194304]{0:T(1024)(128)(4,1)S(1)}, s32[]{:S(2)}) async-start(s8[6291456]{0:T(1024)(128)(4,1)} %bitcast.129), calls=%async_computation.6 | async-start | bytes 8388608 | tf_op jit(solution)/shard_map/while
  236.7 3.1 slice-start.4
  252.6 18.4 %slice-start = ((s8[12582912]{0:T(1024)(128)(4,1)}), s8[4194304]{0:T(1024)(128)(4,1)S(1)}, s32[]{:S(2)}) async-start(s8[12582912]{0:T(1024)(128)(4,1)} %bitcast.125), calls=%async_computation.3 | async-start | bytes 8388608 | tf_op jit(solution)/shard_map/while
  252.6 18.4 %slice-start.1 = ((s8[12582912]{0:T(1024)(128)(4,1)}), s8[4194304]{0:T(1024)(128)(4,1)S(1)}, s32[]{:S(2)}) async-start(s8[12582912]{0:T(1024)(128)(4,1)} %bitcast.125), calls=%async_computation.4 | async-start | bytes 8388608 | tf_op jit(solution)/shard_map/while
  265.1 5.9 %slice-start.2 = ((s8[12582912]{0:T(1024)(128)(4,1)}), s8[4194304]{0:T(1024)(128)(4,1)S(1)}, s32[]{:S(2)}) async-start(s8[12582912]{0:T(1024)(128)(4,1)} %bitcast.125), calls=%async_computation.5 | async-start | bytes 8388608 | tf_op jit(solution)/shard_map/while
  279.2 4.5 copy-start
  284.1 7.0 %slice-start.3 = ((s8[6291456]{0:T(1024)(128)(4,1)}), s8[4194304]{0:T(1024)(128)(4,1)S(1)}, s32[]{:S(2)}) async-start(s8[6291456]{0:T(1024)(128)(4,1)} %bitcast.129), calls=%async_computation.6 | async-start | bytes 8388608 | tf_op jit(solution)/shard_map/while
  288.1 3.1 slice-start.4
  304.0 18.4 %slice-start = ((s8[12582912]{0:T(1024)(128)(4,1)}), s8[4194304]{0:T(1024)(128)(4,1)S(1)}, s32[]{:S(2)}) async-start(s8[12582912]{0:T(1024)(128)(4,1)} %bitcast.125), calls=%async_computation.3 | async-start | bytes 8388608 | tf_op jit(solution)/shard_map/while
  304.0 18.4 %slice-start.1 = ((s8[12582912]{0:T(1024)(128)(4,1)}), s8[4194304]{0:T(1024)(128)(4,1)S(1)}, s32[]{:S(2)}) async-start(s8[12582912]{0:T(1024)(128)(4,1)} %bitcast.125), calls=%async_computation.4 | async-start | bytes 8388608 | tf_op jit(solution)/shard_map/while
  316.5 5.9 %slice-start.2 = ((s8[12582912]{0:T(1024)(128)(4,1)}), s8[4194304]{0:T(1024)(128)(4,1)S(1)}, s32[]{:S(2)}) async-start(s8[12582912]{0:T(1024)(128)(4,1)} %bitcast.125), calls=%async_computation.5 | async-start | bytes 8388608 | tf_op jit(solution)/shard_map/while
  330.6 4.5 copy-start
  351.3 0.7 copy-start.1
Sparse Core Ops, SparseCore 0:
  9.8 50.2 all-gather.3
  62.0 44.6 all-gather.5
  351.5 156.0 all-reduce.5
where the time goes:
time: 521 us; the launch traced here: 520 us
  waiting for transfers between devices  205 us (39%)
  matrix products  137 us (26%)
  local copies, waits for them, and re-layouts  83.2 us (16%)
  blocking collectives  45.5 us (9%)
  other arithmetic  32.9 us (6%)
  between operations  14.5 us (3%)
    unnamed x4, waiting for transfers between devices  130 us
    while x64, local copies, waits for them, and re-layouts  63.1 us
    dot_general x4, matrix products, accumulate(): jnp.dot(spread, first_part.reshape(slot_total, CB * feature_count), preci...  48.1 us
    all_gather x1, waiting for transfers between devices, on_device(): lax.all_gather(means, 'dp', axis=0, tiled=True)  46.5 us
    dot_general x4, matrix products, accumulate(): jnp.dot(spread, second_part.reshape(slot_total, CB * feature_count), prec...  32.8 us
    all_gather x1, waiting for transfers between devices, on_device(): lax.all_gather(inv_var, 'dp', axis=0, tiled=True)  28.7 us
    unnamed x1, blocking collectives  24.3 us
    all_gather x1, blocking collectives, on_device(): lax.all_gather(log_weight, 'dp', axis=0, tiled=True)  21.3 us
  transfers between devices with their start and end apart: 3, of which 3 were waited for; matrix products, arithmetic and copies ran while one was open for 1% of the time, Pallas kernels for 0%

commit v1 on v0

v1 whole, which is shorter than its diff:
```python
import functools
import math

import jax
import jax.numpy as jnp
from jax import lax
from jax.experimental import pallas as pl
from jax.experimental.pallas import tpu as pltpu
from jax.sharding import PartitionSpec as P

CB = 128
RB = 128
CANDS = 4
MESH = pl.DeviceIdType.MESH
NT = (((1,), (1,)), ((), ()))


def remote(src, dst, sems, at, dev):
    send, recv = sems
    return pltpu.make_async_remote_copy(
        src_ref=src,
        dst_ref=dst,
        send_sem=send.at[at],
        recv_sem=recv.at[at],
        device_id={"dp": dev},
        device_id_type=MESH,
    )


def kernel(
    chips,
    cand,
    logw,
    points,
    means,
    inv_var,
    counts_out,
    first_out,
    second_out,
    loglik_out,
    mv,
    iv,
    x,
    g,
    gc,
    slots,
    resp,
    wt,
    acc,
    acc_c,
    ss,
    ss_c,
    sr,
    sr_c,
    rp,
    rp_c,
    rm,
    rm_c,
    in_sem,
    ap_s,
    ap_r,
    am_s,
    am_r,
    as_s,
    as_r,
    rs_s,
    rs_r,
    rp_s,
    rp_r,
    rm_s,
    rm_r,
):
    feat = means.shape[1]
    blocks = cand.shape[0]
    rows = blocks * RB
    dp = lax.axis_index("dp")
    comp = lax.axis_index("comp")
    owners = lax.axis_size("comp")
    n_dp = 2 * chips
    z, c = dp // 2, lax.rem(dp, 2)
    right = lax.rem(dp + 2, n_dp)
    left = lax.rem(dp + n_dp - 2, n_dp)
    sib = dp + 1 - 2 * c

    def share(offset, core):
        return 2 * lax.rem(z + offset + chips, chips) + core

    load_m = pltpu.make_async_copy(means, mv, in_sem.at[0])
    load_i = pltpu.make_async_copy(inv_var, iv, in_sem.at[1])
    load_p = pltpu.make_async_copy(points, x.at[:, pl.ds(0, feat)], in_sem.at[2])
    load_m.start()
    load_i.start()
    load_p.start()

    barrier = pltpu.get_barrier_semaphore()
    for dev in (left, right, sib):
        pl.semaphore_signal(barrier, inc=1, device_id={"dp": dev}, device_id_type=MESH)

    sent = []

    def send(src, src_c, dst, dst_c, sems, at, dev):
        one = remote(src, dst, sems, (*at, 0), dev)
        two = remote(src_c, dst_c, sems, (*at, 1), dev)
        one.start()
        two.start()
        sent.extend((one, two))

    def got(dst, dst_c, sems, at, dev):
        remote(dst, dst, sems, (*at, 0), dev).wait_recv()
        remote(dst_c, dst_c, sems, (*at, 1), dev).wait_recv()

    plus, minus, across = (ap_s, ap_r), (am_s, am_r), (as_s, as_r)

    def pass_on(sh, j, sems, at, dev):
        send(g.at[sh, j], gc.at[sh, j], g.at[sh, j], gc.at[sh, j], sems, (at, j), dev)

    def arrive(sh, j, sems, at, dev):
        got(g.at[sh, j], gc.at[sh, j], sems, (at, j), dev)

    load_m.wait()
    load_i.wait()
    for j in range(2):
        part = pl.ds(j * CB, CB)
        m = mv[part, :].astype(jnp.float32)
        v = iv[part, :].astype(jnp.float32)
        scaled = v * m
        g[dp, j, :, pl.ds(0, feat)] = scaled.astype(jnp.bfloat16)
        g[dp, j, :, pl.ds(feat, feat)] = (-0.5 * v).astype(jnp.bfloat16)
        term = 0.5 * jnp.sum(jnp.log(v) - scaled * m, axis=1, keepdims=True)
        flat = jnp.transpose(jnp.broadcast_to(term, (CB, CB)))[0:8, :]
        weight = logw[pl.ds(j, 1), :].astype(jnp.float32)
        gc[dp, j] = flat + weight - 0.5 * feat * math.log(2.0 * math.pi)
        if j == 0:
            pl.semaphore_wait(barrier, 3)
        pass_on(dp, j, plus, 0, right)
        pass_on(dp, j, minus, 0, left)
        pass_on(dp, j, across, 0, sib)

    load_p.wait()

    def square(i, carry):
        at = pl.ds(pl.multiple_of(i * RB, RB), RB)
        p = x[at, pl.ds(0, feat)].astype(jnp.float32)
        x[at, pl.ds(feat, feat)] = (p * p).astype(jnp.bfloat16)
        return carry

    lax.fori_loop(0, blocks, square, 0)

    def density(sh):
        base = (sh * owners + comp) * 2
        cols = [
            jnp.transpose(jnp.broadcast_to(gc[sh, j, 0:1, :], (CB, CB))) for j in range(2)
        ]
        lhs = g.at[sh]

        def body(i, carry):
            at = pl.ds(pl.multiple_of(i * 2 * RB, 2 * RB), 2 * RB)
            d = lax.dot_general(
                lhs[...].reshape(2 * CB, 2 * feat),
                x[at, :],
                NT,
                preferred_element_type=jnp.float32,
            )
            for r in range(2):
                n = 2 * i + r
                low = d[0:CB, r * RB : (r + 1) * RB] + cols[0]
                high = d[CB : 2 * CB, r * RB : (r + 1) * RB] + cols[1]
                for s in range(CANDS):
                    named = cand[n, s]
                    slots[n, s] = jnp.where(
                        named == base, low, jnp.where(named == base + 1, high, slots[n, s])
                    )
            return carry

        lax.fori_loop(0, blocks // 2, body, 0)

    far = chips // 2
    across_plus, across_minus = 1, 1 + far

    def hop_blocks(h, first):
        return (0, 1) if h < far - 1 else ((0,) if first else (1,))

    def receive(h, j):
        up, down = share(-1 - h, c), share(1 + h, c)
        if j in hop_blocks(h, True):
            arrive(up, j, plus, h, right)
            if h + 1 < far and j in hop_blocks(h + 1, True):
                pass_on(up, j, plus, h + 1, right)
            pass_on(up, j, across, across_plus + h, sib)
        if j in hop_blocks(h, False):
            arrive(down, j, minus, h, left)
            if h + 1 < far and j in hop_blocks(h + 1, False):
                pass_on(down, j, minus, h + 1, left)
            pass_on(down, j, across, across_minus + h, sib)

    def from_sib(h, first):
        sh = share(-1 - h, 1 - c) if first else share(1 + h, 1 - c)
        for j in hop_blocks(h, first):
            arrive(sh, j, across, (across_plus if first else across_minus) + h, sib)
        return sh

    density(dp)
    for j in range(2):
        arrive(sib, j, across, 0, sib)
    receive(0, 0)
    density(sib)
    receive(0, 1)
    for h in range(far - 1):
        density(share(-1 - h, c))
        density(share(1 + h, c))
        if h + 1 < far - 1:
            receive(h + 1, 0)
        density(from_sib(h, True))
        if h + 1 == far - 1:
            receive(h + 1, 0)
            receive(h + 1, 1)
        density(from_sib(h, False))
        if h + 1 < far - 1:
            receive(h + 1, 1)
    density(share(far, c))
    from_sib(far - 1, False)
    density(from_sib(far - 1, True))

    def soften(n, carry):
        d = slots[n]
        peak = jnp.max(jnp.max(d, axis=0), axis=0, keepdims=True)
        e = jnp.exp(d - peak[None])
        total = jnp.sum(jnp.sum(e, axis=0), axis=0, keepdims=True)
        loglik_out[pl.ds(n, 1), :] = (peak + jnp.log(total)) / feat
        resp[n, pl.ds(0, CANDS)] = (e * (1.0 / total)[None]).astype(jnp.bfloat16)
        resp[n, CANDS] = jnp.zeros((CB, RB), jnp.bfloat16)
        return carry

    lax.fori_loop(0, blocks, soften, 0)

    ones = jnp.ones((16, rows), jnp.bfloat16)
    width = 256 if (2 * feat) % 256 == 0 else 128

    def moments(sh, dst, dst_c):
        base = (sh * owners + comp) * 2

        def fill(n, carry):
            for j in range(2):
                at = jnp.int32(CANDS)
                for s in range(CANDS):
                    at = jnp.where(cand[n, s] == base + j, s, at)
                wt[pl.ds(j * CB, CB), pl.ds(pl.multiple_of(n * RB, RB), RB)] = resp[n, at]
            return carry

        lax.fori_loop(0, blocks, fill, 0)
        total = lax.dot_general(ones, wt[...], NT, preferred_element_type=jnp.float32)
        for j in range(2):
            dst_c[j] = total[:, j * CB : (j + 1) * CB].astype(dst_c.dtype)

        def body(k, carry):
            cut = pl.ds(pl.multiple_of(k * width, width), width)
            m = jnp.dot(wt[...], x[:, cut], preferred_element_type=jnp.float32)
            for j in range(2):
                dst[j, :, cut] = m[j * CB : (j + 1) * CB, :].astype(dst.dtype)
            return carry

        lax.fori_loop(0, 2 * feat // width, body, 0)

    plus, minus, across = (rp_s, rp_r), (rm_s, rm_r), (rs_s, rs_r)
    order = [(far, 0)]
    for away in range(far - 1, 0, -1):
        order += [(away, 1), (away, -1)]
    order += [(0, 0)]
    for i, (away, way) in enumerate(order):
        target = way * away if way else away
        moments(share(target, 1 - c), ss.at[i], ss_c.at[i])
        for j in range(2):
            send(ss.at[i, j], ss_c.at[i, j], sr.at[i, j], sr_c.at[i, j], across, (i, j), sib)
        moments(share(target, c), acc, acc_c)
        level = far - away
        for j in (0, 1) if way < 0 else (1, 0):
            got(sr.at[i, j], sr_c.at[i, j], across, (i, j), sib)
            terms = [(sr.at[i, j], sr_c.at[i, j])]
            if away < far and way >= 0 and (level > 1 or j == 0):
                got(rp.at[level - 1, j], rp_c.at[level - 1, j], plus, (level - 1, j), right)
                terms.append((rp.at[level - 1, j], rp_c.at[level - 1, j]))
            if away < far and way <= 0 and (level > 1 or j == 1):
                got(rm.at[level - 1, j], rm_c.at[level - 1, j], minus, (level - 1, j), left)
                terms.append((rm.at[level - 1, j], rm_c.at[level - 1, j]))
            part = pl.ds(j * CB, CB)
            count = acc_c[j]
            for _, t in terms:
                count = count + t[...].astype(jnp.float32)
            if away:
                sr_c[i, j] = count.astype(jnp.bfloat16)
            else:
                counts_out[pl.ds(j, 1), :] = count[0:1, :]

            def add(r, carry, j=j, i=i, terms=terms, away=away):
                here = pl.ds(pl.multiple_of(r * 16, 16), 16)
                t = acc[j, here, :]
                for term, _ in terms:
                    t = t + term[here, :].astype(jnp.float32)
                if away:
                    sr[i, j, here, :] = t.astype(jnp.bfloat16)
                else:
                    there = pl.ds(pl.multiple_of(j * CB + r * 16, 16), 16)
                    first_out[there, :] = t[:, :feat]
                    second_out[there, :] = t[:, feat:]
                return carry

            lax.fori_loop(0, CB // 16, add, 0)
            if away == 0:
                continue
            up = way > 0 or (way == 0 and j == 0)
            dst, dst_c = (rp, rp_c) if up else (rm, rm_c)
            send(
                sr.at[i, j],
                sr_c.at[i, j],
                dst.at[level, j],
                dst_c.at[level, j],
                plus if up else minus,
                (level, j),
                right if up else left,
            )

    for copy in sent:
        copy.wait_send()


def on_device(points, candidates, means, inv_var, log_weight):
    rows, feat = points.shape
    blocks = candidates.shape[0]
    n_dp = lax.axis_size("dp")
    chips = n_dp // 2
    far = chips // 2
    any_space = pl.BlockSpec(memory_space=pl.ANY)
    vmem = pl.BlockSpec(memory_space=pltpu.VMEM)
    bf16, f32 = jnp.bfloat16, jnp.float32
    sem = pltpu.SemaphoreType.DMA
    wide = 2 * feat
    counts, first, second, loglik = pl.pallas_call(
        functools.partial(kernel, chips),
        out_shape=(
            jax.ShapeDtypeStruct((2, CB), f32),
            jax.ShapeDtypeStruct((2 * CB, feat), f32),
            jax.ShapeDtypeStruct((2 * CB, feat), f32),
            jax.ShapeDtypeStruct((blocks, RB), f32),
        ),
        in_specs=[
            pl.BlockSpec(memory_space=pltpu.SMEM),
            vmem,
            any_space,
            any_space,
            any_space,
        ],
        out_specs=(vmem, vmem, vmem, vmem),
        scratch_shapes=[
            pltpu.VMEM((2 * CB, feat), bf16),
            pltpu.VMEM((2 * CB, feat), bf16),
            pltpu.VMEM((rows, wide), bf16),
            pltpu.VMEM((n_dp, 2, CB, wide), bf16),
            pltpu.VMEM((n_dp, 2, 8, CB), f32),
            pltpu.VMEM((blocks, CANDS, CB, RB), f32),
            pltpu.VMEM((blocks, CANDS + 1, CB, RB), bf16),
            pltpu.VMEM((2 * CB, rows), bf16),
            pltpu.VMEM((2, CB, wide), f32),
            pltpu.VMEM((2, 16, CB), f32),
            pltpu.VMEM((chips, 2, CB, wide), bf16),
            pltpu.VMEM((chips, 2, 16, CB), bf16),
            pltpu.VMEM((chips, 2, CB, wide), bf16),
            pltpu.VMEM((chips, 2, 16, CB), bf16),
            pltpu.VMEM((far, 2, CB, wide), bf16),
            pltpu.VMEM((far, 2, 16, CB), bf16),
            pltpu.VMEM((far, 2, CB, wide), bf16),
            pltpu.VMEM((far, 2, 16, CB), bf16),
            sem((3,)),
            sem((far, 2, 2)),
            sem((far, 2, 2)),
            sem((far, 2, 2)),
            sem((far, 2, 2)),
            sem((chips + 1, 2, 2)),
            sem((chips + 1, 2, 2)),
            sem((chips, 2, 2)),
            sem((chips, 2, 2)),
            sem((far, 2, 2)),
            sem((far, 2, 2)),
            sem((far, 2, 2)),
            sem((far, 2, 2)),
        ],
        compiler_params=pltpu.CompilerParams(
            collective_id=0, has_side_effects=True, vmem_limit_bytes=60 * 2**20
        ),
        cost_estimate=pl.CostEstimate(
            flops=4 * rows * n_dp * 2 * CB * wide,
            bytes_accessed=(rows + 8 * CB) * feat * 2,
            transcendentals=rows * CANDS * CB,
        ),
    )(candidates, log_weight.reshape(2, CB), points, means, inv_var)
    return (counts.reshape(-1), first, second, loglik.reshape(-1))


def solution(mesh):
    rows = P(("dp", "comp"))
    wide = P(("dp", "comp"), None)
    return jax.shard_map(
        on_device,
        mesh=mesh,
        in_specs=(wide, wide, wide, wide, rows),
        out_specs=(rows, wide, wide, rows),
        check_vma=False,
    )
```

time: 521 us -> 172 us (0.33)
  waiting for transfers between devices: 205 us -> 0 us
  Pallas kernels: 0 us -> 163 us
  matrix products: 137 us -> 0 us
  local copies, waits for them, and re-layouts: 83.2 us -> 7.32 us
  blocking collectives: 45.5 us -> 0 us
  other arithmetic: 32.9 us -> 0 us
  between operations: 14.5 us -> 0.65 us
    pallas_call x0 -> x1, Pallas kernels: none -> 163 us  [on_device(): pl.pallas_call(functools.partial(kernel, chips), out_shape=(jax.ShapeDtyp...]
    dot_general x40 -> x0, matrix products: 137 us -> none  [the longest x4 48.1 us: accumulate(): jnp.dot(spread, first_part.reshape(slot_total, CB * feature_count), preci...]
    unnamed x4 -> x0, waiting for transfers between devices: 130 us -> none
    all_gather x2 -> x0, waiting for transfers between devices: 75.2 us -> none  [the longest x1 46.5 us: on_device(): lax.all_gather(means, 'dp', axis=0, tiled=True)]
    while x64 -> x0, local copies, waits for them, and re-layouts: 63.1 us -> none
    unnamed x1 -> x0, blocking collectives: 24.3 us -> none
    all_gather x1 -> x0, blocking collectives: 21.3 us -> none  [on_device(): lax.all_gather(log_weight, 'dp', axis=0, tiled=True)]
    reshape x4 -> x0, local copies, waits for them, and re-layouts: 17.7 us -> none  [the longest x1 7.31 us: on_device(): inverse_flat = all_inverse.reshape(group_blocks, CB * feature_count)]
  transfers between devices with their start and end apart: 3 -> 0, of which waited for: 3 -> 0; matrix products, arithmetic and copies ran while one was open for 1% -> 0% of each run, Pallas kernels for 0% -> 0%
where the time goes in v1:
time: 172 us; the launch traced here: 171 us
  Pallas kernels  163 us (95%)
  local copies, waits for them, and re-layouts  7.32 us (4%)
    pallas_call x1, Pallas kernels, on_device(): pl.pallas_call(functools.partial(kernel, chips), out_shape=(jax.ShapeDtyp...  163 us
    unnamed x7, local copies, waits for them, and re-layouts  7.32 us

profile of v1, /device:TPU:1, one launch (start us, length us, event | category | flops | bytes accessed | tf_op | source)
XLA Modules:
  0.0 171.4 jit_solution(8879119951336753274)
XLA Ops:
  0.6 1.4 copy.9.cand
  2.0 163.4 %shard_map.84 = (f32[2,128]{1,0:T(2,128)}, f32[256,768]{1,0:T(8,128)}, f32[256,768]{1,0:T(8,128)}, f32[16,128]{1,0:T(8,128)}) custom-call(s32[16,4]{1,0:T(8,128)} %copy.9.cand, bf16[2,128]{1,0:T(2,128)(2,1)} %bitcast.5, bf16[2048,768]{1,0:T(8,128)(2,1)} %points.1, bf16[256,768]{1,0:T(8,128)(2,1)} %means.1, bf16[256,768]{1,0:T(8,128)(2,1)} %inv_var.1), custom_call_target="tpu_custom_call" | custom-call | flops 51539607552 | bytes 4718592 | tf_op jit(solution)/shard_map/pallas_call | solution.py:337
  165.4 0.0 copy-start
  165.4 1.2 copy.14
  166.7 2.1 %copy.15 = f32[256,768]{1,0:T(8,128)} copy(f32[256,768]{1,0:T(8,128)} %get-tuple-element.17) | data formatting | bytes 1572864
  168.7 2.1 %copy.16 = f32[256,768]{1,0:T(8,128)} copy(f32[256,768]{1,0:T(8,128)} %get-tuple-element.18) | data formatting | bytes 1572864
  170.8 0.0 copy-done
  170.8 0.6 copy.17
Async XLA Ops:
  165.4 5.4 %copy-start = (f32[16,128]{1,0:T(8,128)S(1)}, f32[16,128]{1,0:T(8,128)}, u32[]{:S(2)}) copy-start(f32[16,128]{1,0:T(8,128)} %get-tuple-element.11) | copy-start | bytes 24580

commit v2 on v0

v2 whole, which is shorter than its diff:
```python
import functools
import math

import jax
import jax.numpy as jnp
from jax import lax
from jax.experimental import pallas as pl
from jax.experimental.pallas import tpu as pltpu
from jax.sharding import PartitionSpec as P

CB = 128
RB = 128
CANDS = 4
EXTRA = 16
ROW_CHUNK = 1024
MESH = pl.DeviceIdType.MESH
BF16, F32 = jnp.bfloat16, jnp.float32


def kernel(
    chips,
    cand,
    logw,
    points,
    means,
    inv_var,
    counts_out,
    first_out,
    second_out,
    loglik_out,
    mv,
    iv,
    x,
    xt,
    g,
    slots,
    resp,
    wr,
    acc,
    ss,
    sr,
    rr,
    in_sem,
    ag_s,
    ag_r,
    as_s,
    as_r,
    rs_s,
    rs_r,
    rr_s,
    rr_r,
):
    feat = means.shape[1]
    wide = 2 * feat
    blocks = cand.shape[1]
    rows = blocks * RB
    dp = lax.axis_index("dp")
    comp = lax.axis_index("comp")
    owners = lax.axis_size("comp")
    n_dp = 2 * chips
    far = chips // 2
    z, c = dp // 2, lax.rem(dp, 2)
    right = lax.rem(dp + 2, n_dp)
    left = lax.rem(dp + n_dp - 2, n_dp)
    sib = dp + 1 - 2 * c
    ring = (right, left)
    halves = ((0, feat), (feat, feat + EXTRA))

    def share(offset, core):
        return 2 * lax.rem(z + offset + chips, chips) + core

    def remote(src, dst, sems, at, dev):
        return pltpu.make_async_remote_copy(
            src_ref=src,
            dst_ref=dst,
            send_sem=sems[0].at[at],
            recv_sem=sems[1].at[at],
            device_id={"dp": dev},
            device_id_type=MESH,
        )

    load_m = pltpu.make_async_copy(means, mv, in_sem.at[0])
    load_i = pltpu.make_async_copy(inv_var, iv, in_sem.at[1])
    load_p = pltpu.make_async_copy(points, x.at[:, pl.ds(0, feat)], in_sem.at[2])
    load_m.start()
    load_i.start()
    load_p.start()

    barrier = pltpu.get_barrier_semaphore()
    for dev in (left, right, sib):
        pl.semaphore_signal(barrier, inc=1, device_id={"dp": dev}, device_id_type=MESH)

    ring_sems, across = (ag_s, ag_r), (as_s, as_r)

    def start(ref, sems, at, dev):
        remote(ref, ref, sems, at, dev).start()

    def arrive(ref, sems, at):
        remote(ref, ref, sems, at, sib).wait_recv()

    def half(sh, j, p):
        return g.at[sh, j, pl.ds(halves[p][0], halves[p][1])]

    def own_block(j):
        part = pl.ds(j * CB, CB)
        m = mv[part, :].astype(F32)
        v = iv[part, :].astype(F32)
        scaled = v * m
        g[dp, j, pl.ds(0, feat), :] = jnp.transpose(scaled.astype(BF16))
        g[dp, j, pl.ds(feat, feat), :] = jnp.transpose((-0.5 * v).astype(BF16))
        term = jnp.log(v) - scaled * m
        folded = term[:, 0:CB]
        for k in range(1, feat // CB):
            folded = folded + term[:, k * CB : (k + 1) * CB]
        const = 0.5 * jnp.sum(jnp.transpose(folded), axis=0, keepdims=True)
        const = logw[pl.ds(j, 1), :].astype(F32) + const - 0.5 * feat * math.log(2.0 * math.pi)
        high = const.astype(BF16).astype(F32)
        mid = (const - high).astype(BF16).astype(F32)
        low = const - high - mid
        at = lax.broadcasted_iota(jnp.int32, (EXTRA, CB), 0)
        tile = jnp.where(at == 0, high, jnp.where(at == 1, mid, jnp.where(at == 2, low, 0.0)))
        g[dp, j, pl.ds(wide, EXTRA), :] = tile.astype(BF16)
        if j == 0:
            pl.semaphore_wait(barrier, 3)
        start(g.at[dp, j], ring_sems, (0, 0, j), right)
        start(g.at[dp, j], ring_sems, (1, 0, j), left)
        start(g.at[dp, j], across, (0, j), sib)

    load_m.wait()
    load_i.wait()
    own_block(0)
    load_p.wait()

    def spread(i, carry):
        at = pl.ds(pl.multiple_of(i * RB, RB), RB)
        p = x[at, pl.ds(0, feat)]
        pf = p.astype(F32)
        q = (pf * pf).astype(BF16)
        x[at, pl.ds(feat, feat)] = q
        xt[pl.ds(0, feat), at] = jnp.transpose(p)
        xt[pl.ds(feat, feat), at] = jnp.transpose(q)
        xt[pl.ds(wide, EXTRA), at] = jnp.ones((EXTRA, RB), BF16)
        return carry

    lax.fori_loop(0, blocks, spread, 0)
    own_block(1)

    chunk = min(ROW_CHUNK, rows)

    def keep(i, d, bases, consts):
        for r in range(chunk // RB):
            n = i * (chunk // RB) + r
            here = slice(r * RB, (r + 1) * RB)
            low = d[here, 0:CB] + consts[0]
            high = d[here, CB : 2 * CB] + consts[1]
            for s in range(CANDS):
                named = cand[s, n]
                slots[n, s] = jnp.where(
                    named == bases[0], low, jnp.where(named == bases[1], high, slots[n, s])
                )

    def offsets_of(pair):
        bases, consts = [], []
        for sh, j in pair:
            bases.append((sh * owners + comp) * 2 + j)
            tile = g[sh, j, pl.ds(wide, EXTRA), :].astype(F32)
            consts.append(jnp.sum(tile, axis=0, keepdims=True))
        return bases, consts

    def density(pair):
        bases, consts = offsets_of(pair)
        (sh_a, j_a), (sh_b, j_b) = pair

        def body(i, carry):
            at = pl.ds(pl.multiple_of(i * chunk, chunk), chunk)
            cut = pl.ds(0, wide)
            w = jnp.concatenate([g[sh_a, j_a, cut, :], g[sh_b, j_b, cut, :]], axis=1)
            keep(i, jnp.dot(x[at, :], w, preferred_element_type=F32), bases, consts)
            return carry

        lax.fori_loop(0, rows // chunk, body, 0)

    def density_half(sh, p, store):
        cut = pl.ds(pl.multiple_of(p * feat, feat), feat)

        def body(i, carry):
            at = pl.ds(pl.multiple_of(i * chunk, chunk), chunk)
            kept = pl.ds(pl.multiple_of(store * rows + i * chunk, chunk), chunk)
            w = jnp.concatenate([g[sh, 0, cut, :], g[sh, 1, cut, :]], axis=1)
            d = jnp.dot(x[at, cut], w, preferred_element_type=F32)

            @pl.when(p == 0)
            def _():
                acc[kept, :] = d

            @pl.when(p == 1)
            def _():
                keep(i, d + acc[kept, :], *offsets_of(((sh, 0), (sh, 1))))

            return carry

        lax.fori_loop(0, rows // chunk, body, 0)

    def block_of(way, h, e):
        return e if way == 0 else jnp.where(h == 0, e, 1 - e)

    def hop_share(way, h, core):
        return share(-1 - h if way == 0 else 1 + h, core)

    def pair_of(h, e, core):
        return [(hop_share(way, h, core), block_of(way, h, e)) for way in range(2)]

    def receive(h, e):
        for way, (sh, j) in enumerate(pair_of(h, e, c)):
            arrive(g.at[sh, j], ring_sems, (way, h, j))

            @pl.when(h + 1 < far - 1)
            def _(way=way, sh=sh, j=j):
                start(g.at[sh, j], ring_sems, (way, h + 1, j), ring[way])

            @pl.when((h + 1 == far - 1) & (j == way))
            def _(way=way, sh=sh):
                for p in range(2):
                    start(half(sh, way, p), ring_sems, (way, far - 1, p), ring[way])

            start(g.at[sh, j], across, (1 + way * far + h, j), sib)

    def early(t, carry):
        h, e = (t + 1) // 2 - 1, lax.rem(t + 1, 2)

        def one(k, carry):
            core = jnp.where(k == 0, c, 1 - c)
            own = jnp.where(k == 0, dp, sib)
            pair = [
                (jnp.where(t == 0, own, sh), jnp.where(t == 0, way, j))
                for way, (sh, j) in enumerate(pair_of(h, e, core))
            ]

            @pl.when(k == 1)
            def _():
                for way, (sh, j) in enumerate(pair):
                    at = jnp.where(t == 0, 0, 1 + way * far + h)
                    arrive(g.at[sh, j], across, (at, j))

            density(pair)

            @pl.when((k == 0) & (t < 2 * far - 2))
            def _():
                receive(t // 2, lax.rem(t, 2))

            return carry

        lax.fori_loop(0, 2, one, 0)
        return carry

    lax.fori_loop(0, 2 * far - 1, early, 0)

    def late(p, carry):
        sh = share(far, c)
        for part in range(2):

            @pl.when(p == part)
            def _(part=part):
                for way in range(2):
                    arrive(half(sh, way, part), ring_sems, (way, far - 1, part))
                    start(half(sh, way, part), across, (1 + way * far + far - 1, part), sib)

        def one(k, carry):
            target = share(far, jnp.where(k == 0, c, 1 - c))
            for part in range(2):

                @pl.when((k == 1) & (p == part))
                def _(part=part):
                    for way in range(2):
                        at = (1 + way * far + far - 1, part)
                        arrive(half(target, way, part), across, at)

            density_half(target, p, k)
            return carry

        lax.fori_loop(0, 2, one, 0)
        return carry

    lax.fori_loop(0, 2, late, 0)

    def soften(n):
        d = [slots[n, s] for s in range(CANDS)]
        peak = jnp.max(
            jnp.maximum(jnp.maximum(d[0], d[1]), jnp.maximum(d[2], d[3])), axis=1, keepdims=True
        )
        e = [jnp.exp(v - peak) for v in d]
        total = jnp.sum((e[0] + e[1]) + (e[2] + e[3]), axis=1, keepdims=True)
        scale = 1.0 / total
        for s in range(CANDS):
            resp[n, s] = (e[s] * scale).astype(BF16)
        resp[n, CANDS] = jnp.zeros((RB, CB), BF16)
        slots[n, 0] = jnp.broadcast_to(peak + jnp.log(total), (RB, CB))

    def soften_some(i, carry):
        for k in range(4):
            soften(4 * i + k)
        return carry

    lax.fori_loop(0, blocks // 4, soften_some, 0)

    def sent():
        for way in range(2):
            for h in range(far):
                for p in range(2):
                    ref = g.at[0, 0] if h < far - 1 else half(0, 0, p)
                    remote(ref, ref, ring_sems, (way, h, p), sib).wait_send()
                    remote(ref, ref, across, (1 + way * far + h, p), sib).wait_send()
        for j in range(2):
            remote(g.at[0, 0], g.at[0, 0], across, (0, j), sib).wait_send()

    room = acc.shape[0] // 4
    sum_sems, pair_sems = (rr_s, rr_r), (rs_s, rs_r)
    part = feat // 2

    def fill(k, lv):
        way, core = k // 2, jnp.where(lax.rem(k, 2) == 0, 1 - c, c)
        sh = share(jnp.where(way == 0, far - lv, lv - far), core)
        base = (sh * owners + comp) * 2

        def body(n, carry):
            for j in range(2):
                pick = jnp.int32(CANDS)
                for s in range(CANDS):
                    pick = jnp.where(cand[s, n] == base + j, s, pick)
                here = pl.ds(pl.multiple_of(n * RB, RB), RB)
                wr[k, here, pl.ds(j * CB, CB)] = resp[n, pick]
            return carry

        lax.fori_loop(0, blocks, body, 0)

    def place(sub):
        return pl.ds(pl.multiple_of(sub * part, part), part) if sub is not None else pl.ds(feat, EXTRA)

    def ss_copy(s, way, q, sub):
        at = (2 * s + way, 2 if sub is None else sub)
        return remote(
            ss.at[2 * way + q, place(sub)], sr.at[2 * s + way, place(sub)], pair_sems, at, sib
        )

    def rr_copy(s, way, q, sub):
        lv = (s + 1) // 2
        at = (way, lv, q, 2 if sub is None else sub)
        return remote(
            sr.at[2 * s + way, place(sub)], rr.at[way, lv, q, place(sub)], sum_sems, at, ring[way]
        )

    def on_way(way, act):
        for w in range(2):

            @pl.when(way == w)
            def _(w=w):
                act(w)

    def step(s, carry):
        lv, e = (s + 1) // 2, lax.rem(s + 1, 2)

        @pl.when((s == 0) | (e == 0))
        def _():
            def body(k, carry):
                fill(k, lv)
                return carry

            lax.fori_loop(0, 4, body, 0)

        def one(k, carry):
            core, sub, way = lax.rem(k // 2, 2), k // 4, lax.rem(k, 2)
            q = jnp.where(e == 1, way, 1 - way)
            slot = 2 * way + q

            def product(low, size):
                return jnp.dot(
                    xt[pl.ds(low, size), :], wr[2 * way + core], preferred_element_type=F32
                )

            def put(value, where):
                @pl.when(core == 0)
                def _():
                    @pl.when(s >= 2)
                    def _():
                        ss_copy(s - 2, way, q, where).wait_send()

                    ss[slot, place(where), :] = value.astype(BF16)
                    ss_copy(s, way, q, where).start()

                @pl.when(core == 1)
                def _():
                    start = sub * part if where is not None else feat
                    acc[pl.ds(pl.multiple_of(slot * room + start, 16), value.shape[0]), :] = value

            put(product(pl.multiple_of(q * feat + sub * part, part), part), sub)

            @pl.when((q == 1) & (sub == 1))
            def _():
                put(product(wide, EXTRA), None)

            def combine(where, tile, count):
                ss_copy(s, way, q, where).wait_recv()
                level = lv - 1

                def add(extra):
                    def body(r, carry):
                        start = (sub * part if where is not None else feat) + r * tile
                        start = pl.multiple_of(start, 16)
                        here = pl.ds(start, tile)
                        t = acc[pl.ds(pl.multiple_of(slot * room + start, 16), tile), :]
                        t = t + sr[2 * s + way, here, :].astype(F32)
                        if extra:
                            t = t + rr[way, level, q, here, :].astype(F32)
                        sr[2 * s + way, here, :] = t.astype(BF16)
                        return carry

                    lax.fori_loop(0, count, body, 0)

                @pl.when(s < 2)
                def _():
                    add(False)

                @pl.when((s >= 2) & (lv < far))
                def _():
                    before = jnp.where(s == 2, 0, s - 2)
                    on_way(way, lambda w: rr_copy(before, w, q, where).wait_recv())
                    add(True)

                @pl.when(lv < far)
                def _():
                    on_way(way, lambda w: rr_copy(s, w, q, where).start())

            @pl.when(core == 1)
            def _():
                count = max(k for k in range(1, 9) if part // 16 % k == 0)
                combine(sub, 16 * count, part // (16 * count))

                @pl.when((q == 1) & (sub == 1))
                def _():
                    combine(None, EXTRA, 1)

            return carry

        lax.fori_loop(0, 8, one, 0)

        @pl.when(s == 1)
        def _():
            def out(n, carry):
                norm = jnp.transpose(slots[n, 0])[0:1, :]
                loglik_out[pl.ds(n, 1), :] = norm / feat
                return carry

            lax.fori_loop(0, blocks, out, 0)

        return carry

    lax.fori_loop(0, 2 * far, step, 0)

    last = 2 * far - 1

    def final_of(q, start, size):
        way = 1 - q
        t = acc[pl.ds((2 * way + q) * room + start, size), :]
        t = t + sr[2 * last + way, pl.ds(start, size), :].astype(F32)
        for w in range(2):
            t = t + rr[w, far - 1, q, pl.ds(start, size), :].astype(F32)
        return t

    def done(q, sub):
        for w in range(2):
            rr_copy(last - 1 if q == w else last - 2, w, q, sub).wait_recv()

    for sub in range(2):
        for q in range(2):
            done(q, sub)
            out = second_out if q else first_out
            edges = list(range(sub * part, (sub + 1) * part, min(CB, part)))
            for low in edges:
                t = final_of(q, low, min(CB, part))
                out[:, pl.ds(low, min(CB, part))] = jnp.transpose(t)
    done(1, None)
    t = final_of(1, feat, EXTRA)
    for j in range(2):
        counts_out[pl.ds(j, 1), :] = t[0:1, j * CB : (j + 1) * CB]

    sent()
    for s in range(2 * far):
        for way in range(2):
            q = way if s % 2 == 0 else 1 - way
            for sub in (0, 1) if q == 0 else (0, 1, None):
                if s >= last - 1:
                    ss_copy(s, way, q, sub).wait_send()
                if s < last:
                    rr_copy(s, way, q, sub).wait_send()


def on_device(points, candidates, means, inv_var, log_weight):
    rows, feat = points.shape
    blocks = candidates.shape[0]
    n_dp = lax.axis_size("dp")
    chips = n_dp // 2
    far = chips // 2
    any_space = pl.BlockSpec(memory_space=pl.ANY)
    vmem = pl.BlockSpec(memory_space=pltpu.VMEM)
    sem = pltpu.SemaphoreType.DMA
    wide = 2 * feat
    full = wide + EXTRA
    most = feat + EXTRA
    units = 4 * far
    shapes = (
        jax.ShapeDtypeStruct((2, CB), F32),
        jax.ShapeDtypeStruct((2 * CB, feat), F32),
        jax.ShapeDtypeStruct((2 * CB, feat), F32),
        jax.ShapeDtypeStruct((blocks, RB), F32),
    )
    results = pl.pallas_call(
        functools.partial(kernel, chips),
        out_shape=tuple(pltpu.VMEM(shape.shape, F32) for shape in shapes),
        in_specs=[
            pl.BlockSpec(memory_space=pltpu.SMEM),
            vmem,
            any_space,
            any_space,
            any_space,
        ],
        out_specs=(vmem, vmem, vmem, vmem),
        scratch_shapes=[
            pltpu.VMEM((2 * CB, feat), BF16),
            pltpu.VMEM((2 * CB, feat), BF16),
            pltpu.VMEM((rows, wide), BF16),
            pltpu.VMEM((full, rows), BF16),
            pltpu.VMEM((n_dp, 2, full, CB), BF16),
            pltpu.VMEM((blocks, CANDS, RB, CB), F32),
            pltpu.VMEM((blocks, CANDS + 1, RB, CB), BF16),
            pltpu.VMEM((4, rows, 2 * CB), BF16),
            pltpu.VMEM((max(2 * rows, 4 * most), 2 * CB), F32),
            pltpu.VMEM((4, most, 2 * CB), BF16),
            pltpu.VMEM((units, most, 2 * CB), BF16),
            pltpu.VMEM((2, far, 2, most, 2 * CB), BF16),
            sem((3,)),
            sem((2, far, 2)),
            sem((2, far, 2)),
            sem((chips + 1, 2)),
            sem((chips + 1, 2)),
            sem((units, 3)),
            sem((units, 3)),
            sem((2, far, 2, 3)),
            sem((2, far, 2, 3)),
        ],
        compiler_params=pltpu.CompilerParams(
            collective_id=0, has_side_effects=True, vmem_limit_bytes=60 * 2**20
        ),
        cost_estimate=pl.CostEstimate(
            flops=4 * rows * n_dp * 2 * CB * wide,
            bytes_accessed=(rows + 8 * CB) * feat * 2,
            transcendentals=rows * CANDS * CB,
        ),
    )(candidates.T, log_weight.reshape(2, CB), points, means, inv_var)
    counts, first, second, loglik = results
    return (counts.reshape(-1), first, second, loglik.reshape(-1))


def solution(mesh):
    rows = P(("dp", "comp"))
    wide = P(("dp", "comp"), None)
    return jax.shard_map(
        on_device,
        mesh=mesh,
        in_specs=(wide, wide, wide, wide, rows),
        out_specs=(rows, wide, wide, rows),
        check_vma=False,
    )
```

time: 521 us -> 149 us (0.29)
  waiting for transfers between devices: 205 us -> 0 us
  Pallas kernels: 0 us -> 145 us
  matrix products: 137 us -> 0 us
  local copies, waits for them, and re-layouts: 83.2 us -> 2.92 us
  blocking collectives: 45.5 us -> 0 us
  other arithmetic: 32.9 us -> 0 us
  between operations: 14.5 us -> 0.64 us
    pallas_call x0 -> x1, Pallas kernels: none -> 145 us  [on_device(): pl.pallas_call(functools.partial(kernel, chips), out_shape=tuple((pltpu.V...]
    dot_general x40 -> x0, matrix products: 137 us -> none  [the longest x4 48.1 us: accumulate(): jnp.dot(spread, first_part.reshape(slot_total, CB * feature_count), preci...]
    unnamed x4 -> x0, waiting for transfers between devices: 130 us -> none
    all_gather x2 -> x0, waiting for transfers between devices: 75.2 us -> none  [the longest x1 46.5 us: on_device(): lax.all_gather(means, 'dp', axis=0, tiled=True)]
    while x64 -> x0, local copies, waits for them, and re-layouts: 63.1 us -> none
    unnamed x1 -> x0, blocking collectives: 24.3 us -> none
    all_gather x1 -> x0, blocking collectives: 21.3 us -> none  [on_device(): lax.all_gather(log_weight, 'dp', axis=0, tiled=True)]
    reshape x4 -> x0, local copies, waits for them, and re-layouts: 17.7 us -> none  [the longest x1 7.31 us: on_device(): inverse_flat = all_inverse.reshape(group_blocks, CB * feature_count)]
  transfers between devices with their start and end apart: 3 -> 0, of which waited for: 3 -> 0; matrix products, arithmetic and copies ran while one was open for 1% -> 0% of each run, Pallas kernels for 0% -> 0%
where the time goes in v2:
time: 149 us
  Pallas kernels  145 us (97%)
  local copies, waits for them, and re-layouts  2.92 us (2%)
    pallas_call x1, Pallas kernels, on_device(): pl.pallas_call(functools.partial(kernel, chips), out_shape=tuple((pltpu.V...  145 us

profile of v2, /device:TPU:1, one launch (start us, length us, event | category | flops | bytes accessed | tf_op | source)
XLA Modules:
  0.0 148.6 jit_solution(10942458630598850465)
XLA Ops:
  0.6 145.0 %shard_map.84 = (f32[2,128]{1,0:T(2,128)S(1)}, f32[256,768]{1,0:T(8,128)S(1)}, f32[256,768]{1,0:T(8,128)S(1)}, f32[16,128]{1,0:T(8,128)S(1)}) custom-call(s32[4,16]{1,0:T(4,128)} %bitcast.6, bf16[2,128]{1,0:T(2,128)(2,1)} %bitcast.7, bf16[2048,768]{1,0:T(8,128)(2,1)} %points.1, bf16[256,768]{1,0:T(8,128)(2,1)} %means.1, bf16[256,768]{1,0:T(8,128)(2,1)} %inv_var.1), custom_call_target="tpu_custom_call" | custom-call | flops 51539607552 | bytes 4718592 | tf_op jit(solution)/shard_map/pallas_call | solution.py:516
  145.7 0.6 copy.13
  146.2 0.6 copy.16
  146.8 0.9 copy.14
  147.7 0.9 copy.15

commit v3 on v2

--- a/solution.py
+++ b/solution.py
@@ -358,6 +358,7 @@
 
     def step(s, carry):
         lv, e = (s + 1) // 2, lax.rem(s + 1, 2)
+        shared = (lv == 0) | (lv == far)
 
         @pl.when((s == 0) | (e == 0))
         def _():
@@ -365,7 +366,7 @@
                 fill(k, lv)
                 return carry
 
-            lax.fori_loop(0, 4, body, 0)
+            lax.fori_loop(0, jnp.where(shared, 2, 4), body, 0)
 
         def one(k, carry):
             core, sub, way = lax.rem(k // 2, 2), k // 4, lax.rem(k, 2)
@@ -374,7 +375,7 @@
 
             def product(low, size):
                 return jnp.dot(
-                    xt[pl.ds(low, size), :], wr[2 * way + core], preferred_element_type=F32
+                    xt[pl.ds(low, size), :], wr[jnp.where(shared, core, 2 * way + core)], preferred_element_type=F32
                 )
 
             def put(value, where):
@@ -492,6 +493,17 @@
                     ss_copy(s, way, q, sub).wait_send()
                 if s < last:
                     rr_copy(s, way, q, sub).wait_send()
+
+
+def copy_out(*refs):
+    sources, targets, sems = refs[:4], refs[4:8], refs[8]
+    copies = [
+        pltpu.make_async_copy(s, t, sems.at[i]) for i, (s, t) in enumerate(zip(sources, targets))
+    ]
+    for copy in copies:
+        copy.start()
+    for copy in copies:
+        copy.wait()
 
 
 def on_device(points, candidates, means, inv_var, log_weight):
@@ -556,7 +568,14 @@
             transcendentals=rows * CANDS * CB,
         ),
     )(candidates.T, log_weight.reshape(2, CB), points, means, inv_var)
-    counts, first, second, loglik = results
+    held = [pltpu.with_memory_space_constraint(r, pltpu.VMEM) for r in results]
+    counts, first, second, loglik = pl.pallas_call(
+        copy_out,
+        out_shape=shapes,
+        in_specs=[any_space] * 4,
+        out_specs=(any_space,) * 4,
+        scratch_shapes=[sem((4,))],
+    )(*held)
     return (counts.reshape(-1), first, second, loglik.reshape(-1))
 
 

time: 149 us -> 146 us (0.980)
  local copies, waits for them, and re-layouts: 2.92 us -> 0 us
    unnamed x4 -> x0, local copies, waits for them, and re-layouts: 2.92 us -> none
where the time goes in v3:
time: 146 us
  Pallas kernels  145 us (99%)
    pallas_call x1, Pallas kernels, on_device(): pl.pallas_call(functools.partial(kernel, chips), out_shape=tuple((pltpu.V...  144 us

profile of v3, /device:TPU:1, one launch (start us, length us, event | category | flops | bytes accessed | tf_op | source)
XLA Modules:
  0.0 145.8 jit_solution(2426249540752146202)
XLA Ops:
  0.6 144.0 %shard_map.84 = (f32[2,128]{1,0:T(2,128)S(1)}, f32[256,768]{1,0:T(8,128)S(1)}, f32[256,768]{1,0:T(8,128)S(1)}, f32[16,128]{1,0:T(8,128)S(1)}) custom-call(s32[4,16]{1,0:T(4,128)} %bitcast.5, bf16[2,128]{1,0:T(2,128)(2,1)} %bitcast.7, bf16[2048,768]{1,0:T(8,128)(2,1)} %points.1, bf16[256,768]{1,0:T(8,128)(2,1)} %means.1, bf16[256,768]{1,0:T(8,128)(2,1)} %inv_var.1), custom_call_target="tpu_custom_call" | custom-call | flops 51539607552 | bytes 4718592 | tf_op jit(solution)/shard_map/pallas_call | solution.py:528
  144.6 1.2 shard_map.85

commit v4 on v3

--- a/solution.py
+++ b/solution.py
@@ -315,7 +315,7 @@
 
     room = acc.shape[0] // 4
     sum_sems, pair_sems = (rr_s, rr_r), (rs_s, rs_r)
-    part = feat // 2
+    part = feat // 3
 
     def fill(k, lv):
         way, core = k // 2, jnp.where(lax.rem(k, 2) == 0, 1 - c, c)
@@ -337,14 +337,14 @@
         return pl.ds(pl.multiple_of(sub * part, part), part) if sub is not None else pl.ds(feat, EXTRA)
 
     def ss_copy(s, way, q, sub):
-        at = (2 * s + way, 2 if sub is None else sub)
+        at = (2 * s + way, 3 if sub is None else sub)
         return remote(
             ss.at[2 * way + q, place(sub)], sr.at[2 * s + way, place(sub)], pair_sems, at, sib
         )
 
     def rr_copy(s, way, q, sub):
         lv = (s + 1) // 2
-        at = (way, lv, q, 2 if sub is None else sub)
+        at = (way, lv, q, 3 if sub is None else sub)
         return remote(
             sr.at[2 * s + way, place(sub)], rr.at[way, lv, q, place(sub)], sum_sems, at, ring[way]
         )
@@ -395,7 +395,7 @@
 
             put(product(pl.multiple_of(q * feat + sub * part, part), part), sub)
 
-            @pl.when((q == 1) & (sub == 1))
+            @pl.when((q == 1) & (sub == 2))
             def _():
                 put(product(wide, EXTRA), None)
 
@@ -436,13 +436,13 @@
                 count = max(k for k in range(1, 9) if part // 16 % k == 0)
                 combine(sub, 16 * count, part // (16 * count))
 
-                @pl.when((q == 1) & (sub == 1))
+                @pl.when((q == 1) & (sub == 2))
                 def _():
                     combine(None, EXTRA, 1)
 
             return carry
 
-        lax.fori_loop(0, 8, one, 0)
+        lax.fori_loop(0, 12, one, 0)
 
         @pl.when(s == 1)
         def _():
@@ -471,7 +471,7 @@
         for w in range(2):
             rr_copy(last - 1 if q == w else last - 2, w, q, sub).wait_recv()
 
-    for sub in range(2):
+    for sub in range(3):
         for q in range(2):
             done(q, sub)
             out = second_out if q else first_out
@@ -488,7 +488,7 @@
     for s in range(2 * far):
         for way in range(2):
             q = way if s % 2 == 0 else 1 - way
-            for sub in (0, 1) if q == 0 else (0, 1, None):
+            for sub in (0, 1, 2) if q == 0 else (0, 1, 2, None):
                 if s >= last - 1:
                     ss_copy(s, way, q, sub).wait_send()
                 if s < last:
@@ -554,10 +554,10 @@
             sem((2, far, 2)),
             sem((chips + 1, 2)),
             sem((chips + 1, 2)),
-            sem((units, 3)),
-            sem((units, 3)),
-            sem((2, far, 2, 3)),
-            sem((2, far, 2, 3)),
+            sem((units, 4)),
+            sem((units, 4)),
+            sem((2, far, 2, 4)),
+            sem((2, far, 2, 4)),
         ],
         compiler_params=pltpu.CompilerParams(
             collective_id=0, has_side_effects=True, vmem_limit_bytes=60 * 2**20

time: 146 us -> 146 us (level)
  no operation moved by 1% of the time
where the time goes in v4:
time: 146 us
  Pallas kernels  145 us (99%)
    pallas_call x1, Pallas kernels, on_device(): pl.pallas_call(functools.partial(kernel, chips), out_shape=tuple((pltpu.V...  144 us

profile of v4, /device:TPU:1, one launch (start us, length us, event | category | flops | bytes accessed | tf_op | source)
XLA Modules:
  0.0 146.0 jit_solution(4270745624492907631)
XLA Ops:
  0.6 144.2 %shard_map.84 = (f32[2,128]{1,0:T(2,128)S(1)}, f32[256,768]{1,0:T(8,128)S(1)}, f32[256,768]{1,0:T(8,128)S(1)}, f32[16,128]{1,0:T(8,128)S(1)}) custom-call(s32[4,16]{1,0:T(4,128)} %bitcast.5, bf16[2,128]{1,0:T(2,128)(2,1)} %bitcast.7, bf16[2048,768]{1,0:T(8,128)(2,1)} %points.1, bf16[256,768]{1,0:T(8,128)(2,1)} %means.1, bf16[256,768]{1,0:T(8,128)(2,1)} %inv_var.1), custom_call_target="tpu_custom_call" | custom-call | flops 51539607552 | bytes 4718592 | tf_op jit(solution)/shard_map/pallas_call | solution.py:528
  144.8 1.2 shard_map.85
